TPU v7x, 32 devices: a whole 2x2x4 slice. The times are simulated.
32 devices in a mesh: fsdp: 8 (over z, x), ctx: 2 (over y), tp: 2 (over core).
Axes of the slice: x: 2, y: 2, z: 4, core: 2. Of those that a mesh axis runs over, the one named last changes fastest.
Arguments:
- tokens: bfloat16 [8, 2048, 768], P('fsdp', 'ctx'), may hold values from -6 to 6
- cotangent: float32 [8, 2048, 768], P('fsdp', 'ctx'), may hold values from -6 to 6
- lengths: int32 [8, 4], P('fsdp'), may hold values from 0 to 2048, as said below
- w_qkv: bfloat16 [3, 768, 768], P(None, 'fsdp', 'tp'), may hold values from -0.21875 to 0.21875
- w_out: bfloat16 [768, 768], P('tp', 'fsdp'), may hold values from -3.5 to 3.5
- w_up: bfloat16 [768, 3072], P('fsdp', 'tp'), may hold values from -0.21875 to 0.21875
- w_down: bfloat16 [3072, 768], P('tp', 'fsdp'), may hold values from -0.109375 to 0.109375
- qv_bias: float32 [2, 768], P(None, 'tp'), may hold values from -3 to 3
- up_bias: float32 [3072], P('tp'), may hold values from -3 to 3
- out_bias: float32 [2, 768], replicated, may hold values from -3 to 3
- gains: float32 [2, 768], replicated, may hold values from 0.25 to 1.75
- shifts: float32 [2, 768], replicated, may hold values from -3 to 3
Outputs:
- output: float32 [8, 2048, 768], P('fsdp', 'ctx')
- token_grad: float32 [8, 2048, 768], P('fsdp', 'ctx')
- qkv_grad: float32 [3, 768, 768], P(None, ('fsdp', 'ctx'), 'tp')
- out_proj_grad: float32 [768, 768], P('tp', ('fsdp', 'ctx'))
- up_grad: float32 [768, 3072], P(('fsdp', 'ctx'), 'tp')
- down_grad: float32 [3072, 768], P('tp', ('fsdp', 'ctx'))
- qv_bias_grad: float32 [2, 2, 384], P(None, 'tp', ('fsdp', 'ctx'))
- up_bias_grad: float32 [2, 1536], P('tp', ('fsdp', 'ctx'))
- out_bias_grad: float32 [2, 768], P(None, ('fsdp', 'ctx'))
- gains_grad: float32 [2, 768], P(None, ('fsdp', 'ctx'))
- shifts_grad: float32 [2, 768], P(None, ('fsdp', 'ctx'))
Inputs may be any that keep to these rules, and one draw needn't show every extreme that they name: Each row holds 1 to 4 sequences in its first slots, each of 1024 positions or more, and zeros in the slots after them; the lengths of a row add up to 2048, its sequences follow one another from position 0 in the order given, and at least one row is a single sequence of 2048 positions.
All inputs are finite; a program needn't handle non-finite values.
Results may differ from a plain program's by a relative error of at most 0.015.
Values may be sent and summed in bfloat16 or wider, within the bound.
A program may use at most 192 MiB of HBM per device.

v0:
```python
import math

import jax
import jax.numpy as jnp
from jax import lax
from jax.sharding import PartitionSpec as P

HD = 64


EPSILON = 1e-05
NEG_LARGE = -1e30


def normalize(values):
    centre = values - jnp.mean(values, axis=-1, keepdims=True)
    variance = jnp.mean(centre * centre, axis=-1, keepdims=True)
    inv_std = lax.rsqrt(variance + EPSILON)
    return (centre * inv_std, inv_std)


def norm_back(grad_in, normed, inv_std):
    mean_grad = jnp.mean(grad_in, axis=-1, keepdims=True)
    mean_cross = jnp.mean(grad_in * normed, axis=-1, keepdims=True)
    return inv_std * (grad_in - mean_grad - normed * mean_cross)


def gelu_curve(values):
    return jax.nn.gelu(values, approximate=True)


def per_device(
    tokens,
    cotangent,
    lengths,
    w_qkv,
    w_out,
    w_up,
    w_down,
    qv_bias,
    up_bias,
    out_bias,
    gains,
    shifts,
):
    stream = tokens[0].astype(jnp.float32)
    grad_out = cotangent[0]
    seg_len = stream.shape[0]
    ctx_count = lax.axis_size("ctx")
    ctx_here = lax.axis_index("ctx")
    row_len = seg_len * ctx_count
    first_pos = ctx_here * seg_len
    seq_lens = lengths[0]
    seq_starts = jnp.cumsum(seq_lens, dtype=jnp.int32) - seq_lens

    def doc_of(spots):
        return jnp.sum((spots[:, None] >= seq_starts[None, :]).astype(jnp.int32), axis=1) - 1

    query_pos = first_pos + jnp.arange(seg_len, dtype=jnp.int32)
    query_doc = doc_of(query_pos)
    all_pos = jnp.arange(row_len, dtype=jnp.int32)
    all_doc = doc_of(all_pos)
    local_width = w_qkv.shape[2]
    heads_dev = local_width // HD
    block = math.gcd(row_len, 512)
    block_count = row_len // block
    scale = HD ** (-0.5)
    block_last_doc = all_doc.reshape(block_count, block)[:, block - 1]
    first_block = jnp.sum((block_last_doc < query_doc[0]).astype(jnp.int32))
    end_block = (first_pos + seg_len - 1) // block + 1
    gathered = (
        lax.all_gather(w_qkv, "fsdp", axis=1, tiled=True),
        lax.all_gather(w_out, "fsdp", axis=1, tiled=True),
        lax.all_gather(w_up, "fsdp", axis=0, tiled=True),
        lax.all_gather(w_down, "fsdp", axis=1, tiled=True),
    )
    qkv_full, out_full, up_full, down_full = gathered
    normed, inv_std = normalize(stream)
    hidden = (normed * gains[0] + shifts[0]).astype(jnp.bfloat16)
    projected = jnp.einsum("td,cde->cte", hidden, qkv_full, preferred_element_type=jnp.float32)
    queries = (projected[0] + qv_bias[0]).astype(jnp.bfloat16)
    keys_local = projected[1].astype(jnp.bfloat16)
    values_local = (projected[2] + qv_bias[1]).astype(jnp.bfloat16)
    all_keys, all_values = (
        lax.all_gather(keys_local, "ctx", axis=0, tiled=True),
        lax.all_gather(values_local, "ctx", axis=0, tiled=True),
    )
    query_heads = queries.reshape(seg_len, heads_dev, HD)

    def take_block(source, block_id):
        return lax.dynamic_slice_in_dim(source, block_id * block, block, 0).reshape(
            block, heads_dev, HD
        )

    def block_scores(key_part, block_id):
        key_pos = lax.dynamic_slice_in_dim(all_pos, block_id * block, block, 0)
        key_doc = lax.dynamic_slice_in_dim(all_doc, block_id * block, block, 0)
        scores = (
            jnp.einsum("qhd,khd->hqk", query_heads, key_part, preferred_element_type=jnp.float32)
            * scale
        )
        allowed = (key_pos[None, :] <= query_pos[:, None]) & (
            key_doc[None, :] == query_doc[:, None]
        )
        return (scores, allowed[None])

    def max_step(block_id, running):
        run_max, run_sum = running
        scores, allowed = block_scores(take_block(all_keys, block_id), block_id)
        masked = jnp.where(allowed, scores, NEG_LARGE)
        new_max = jnp.maximum(run_max, jnp.max(masked, axis=-1))
        weights = jnp.where(allowed, jnp.exp(masked - new_max[..., None]), 0.0)
        return (new_max, run_sum * jnp.exp(run_max - new_max) + jnp.sum(weights, axis=-1))

    start_state = (
        jnp.full((heads_dev, seg_len), NEG_LARGE, jnp.float32),
        jnp.zeros((heads_dev, seg_len), jnp.float32),
    )
    run_max, run_sum = lax.fori_loop(first_block, end_block, max_step, start_state)
    log_total = run_max + jnp.log(run_sum)

    def probs_of(scores, allowed):
        return jnp.where(
            allowed, jnp.exp(jnp.where(allowed, scores, NEG_LARGE) - log_total[..., None]), 0.0
        )

    def mix_step(block_id, totals):
        scores, allowed = block_scores(take_block(all_keys, block_id), block_id)
        weights = probs_of(scores, allowed).astype(jnp.bfloat16)
        value_part = take_block(all_values, block_id)
        return totals + jnp.einsum(
            "hqk,khd->hqd", weights, value_part, preferred_element_type=jnp.float32
        )

    mixed_total = lax.fori_loop(
        first_block, end_block, mix_step, jnp.zeros((heads_dev, seg_len, HD), jnp.float32)
    )
    mixed = mixed_total.transpose(1, 0, 2).reshape(seg_len, local_width).astype(jnp.bfloat16)
    partial_attn = jnp.dot(mixed, out_full, preferred_element_type=jnp.float32)
    middle = (
        stream + lax.psum(partial_attn.astype(jnp.bfloat16), "tp").astype(jnp.float32) + out_bias[0]
    )
    normed_two, inv_two = normalize(middle)
    hidden_two = (normed_two * gains[1] + shifts[1]).astype(jnp.bfloat16)
    pre_act = jnp.dot(hidden_two, up_full, preferred_element_type=jnp.float32) + up_bias
    activ_exact, gelu_pull = jax.vjp(gelu_curve, pre_act)
    activ = activ_exact.astype(jnp.bfloat16)
    partial_ff = jnp.dot(activ, down_full, preferred_element_type=jnp.float32)
    output = (
        middle + lax.psum(partial_ff.astype(jnp.bfloat16), "tp").astype(jnp.float32) + out_bias[1]
    )
    qkv_back, out_back, up_back, down_back = (
        lax.all_gather(w_qkv, "fsdp", axis=1, tiled=True),
        lax.all_gather(w_out, "fsdp", axis=1, tiled=True),
        lax.all_gather(w_up, "fsdp", axis=0, tiled=True),
        lax.all_gather(w_down, "fsdp", axis=1, tiled=True),
    )
    down_in = grad_out.astype(jnp.bfloat16)
    act_grad = jnp.einsum("te,fe->tf", down_in, down_back, preferred_element_type=jnp.float32)
    pre_grad = gelu_pull(act_grad)[0].astype(jnp.bfloat16)
    partial_two = jnp.einsum("tf,df->td", pre_grad, up_back, preferred_element_type=jnp.float32)
    hidden_two_grad = lax.psum(partial_two.astype(jnp.bfloat16), "tp").astype(jnp.float32)
    middle_grad = grad_out + norm_back(hidden_two_grad * gains[1], normed_two, inv_two)
    attn_in = middle_grad.astype(jnp.bfloat16)
    mixed_grad = jnp.einsum(
        "te,ce->tc", attn_in, out_back, preferred_element_type=jnp.float32
    ).astype(jnp.bfloat16)
    grad_heads = mixed_grad.reshape(seg_len, heads_dev, HD)
    back_keys, back_values = (
        lax.all_gather(keys_local, "ctx", axis=0, tiled=True),
        lax.all_gather(values_local, "ctx", axis=0, tiled=True),
    )
    delta = jnp.einsum("qhd,hqd->hq", grad_heads.astype(jnp.float32), mixed_total)

    def grad_step(block_id, carry):
        query_total, key_buffer, value_buffer = carry
        key_part = take_block(back_keys, block_id)
        value_part = take_block(back_values, block_id)
        scores, allowed = block_scores(key_part, block_id)
        weights = probs_of(scores, allowed)
        weight_grad = jnp.einsum(
            "qhd,khd->hqk", grad_heads, value_part, preferred_element_type=jnp.float32
        )
        score_grad = (weights * (weight_grad - delta[..., None])).astype(jnp.bfloat16)
        query_total = query_total + jnp.einsum(
            "hqk,khd->hqd", score_grad, key_part, preferred_element_type=jnp.float32
        )
        key_term = (
            jnp.einsum("hqk,qhd->khd", score_grad, query_heads, preferred_element_type=jnp.float32)
            * scale
        )
        value_term = jnp.einsum(
            "hqk,qhd->khd",
            weights.astype(jnp.bfloat16),
            grad_heads,
            preferred_element_type=jnp.float32,
        )
        key_buffer = lax.dynamic_update_slice_in_dim(
            key_buffer, key_term.reshape(block, local_width), block_id * block, 0
        )
        value_buffer = lax.dynamic_update_slice_in_dim(
            value_buffer, value_term.reshape(block, local_width), block_id * block, 0
        )
        return (query_total, key_buffer, value_buffer)

    empty_row = jnp.zeros((row_len, local_width), jnp.float32)
    query_total, key_terms, value_terms = lax.fori_loop(
        first_block,
        end_block,
        grad_step,
        (jnp.zeros((heads_dev, seg_len, HD), jnp.float32), empty_row, empty_row),
    )
    key_grad, value_grad = (
        lax.psum_scatter(
            key_terms.astype(jnp.bfloat16), "ctx", scatter_dimension=0, tiled=True
        ).astype(jnp.float32),
        lax.psum_scatter(
            value_terms.astype(jnp.bfloat16), "ctx", scatter_dimension=0, tiled=True
        ).astype(jnp.float32),
    )
    query_grad = query_total.transpose(1, 0, 2).reshape(seg_len, local_width) * scale
    qkv_grad_in = jnp.stack([query_grad, key_grad, value_grad]).astype(jnp.bfloat16)
    partial_hidden = jnp.einsum(
        "cte,cde->td", qkv_grad_in, qkv_back, preferred_element_type=jnp.float32
    )
    hidden_grad = lax.psum(partial_hidden.astype(jnp.bfloat16), "tp").astype(jnp.float32)
    token_grad = middle_grad + norm_back(hidden_grad * gains[0], normed, inv_std)
    qkv_term = jnp.einsum("td,cte->cde", hidden, qkv_grad_in, preferred_element_type=jnp.float32)
    out_term = jnp.einsum("tc,te->ce", mixed, attn_in, preferred_element_type=jnp.float32)
    up_term = jnp.einsum("td,tf->df", hidden_two, pre_grad, preferred_element_type=jnp.float32)
    down_term = jnp.einsum("tf,te->fe", activ, down_in, preferred_element_type=jnp.float32)
    qv_term = jnp.stack(
        [
            jnp.sum(qkv_grad_in[0].astype(jnp.float32), axis=0),
            jnp.sum(qkv_grad_in[2].astype(jnp.float32), axis=0),
        ]
    )
    up_bias_term = jnp.sum(pre_grad.astype(jnp.float32), axis=0)
    out_bias_term = jnp.stack(
        [jnp.sum(attn_in.astype(jnp.float32), axis=0), jnp.sum(down_in.astype(jnp.float32), axis=0)]
    )
    gains_term = jnp.stack(
        [jnp.sum(hidden_grad * normed, axis=0), jnp.sum(hidden_two_grad * normed_two, axis=0)]
    )
    shifts_term = jnp.stack([jnp.sum(hidden_grad, axis=0), jnp.sum(hidden_two_grad, axis=0)])
    summed = (
        lax.psum_scatter(qkv_term, ("fsdp", "ctx"), scatter_dimension=1, tiled=True),
        lax.psum_scatter(out_term, ("fsdp", "ctx"), scatter_dimension=1, tiled=True),
        lax.psum_scatter(up_term, ("fsdp", "ctx"), scatter_dimension=0, tiled=True),
        lax.psum_scatter(down_term, ("fsdp", "ctx"), scatter_dimension=1, tiled=True),
        lax.psum_scatter(qv_term, ("fsdp", "ctx"), scatter_dimension=1, tiled=True),
        lax.psum_scatter(up_bias_term, ("fsdp", "ctx"), scatter_dimension=0, tiled=True),
        lax.psum_scatter(out_bias_term, ("fsdp", "ctx"), scatter_dimension=1, tiled=True),
        lax.psum_scatter(gains_term, ("fsdp", "ctx"), scatter_dimension=1, tiled=True),
        lax.psum_scatter(shifts_term, ("fsdp", "ctx"), scatter_dimension=1, tiled=True),
    )
    return (
        output[None],
        token_grad[None],
        summed[0],
        summed[1],
        summed[2],
        summed[3],
        summed[4][:, None, :],
        summed[5][None, :],
        summed[6],
        summed[7],
        summed[8],
    )


def solution(mesh):
    placed = (
        P("fsdp", "ctx", None),
        P("fsdp", "ctx", None),
        P("fsdp", None),
        P(None, "fsdp", "tp"),
        P("tp", "fsdp"),
        P("fsdp", "tp"),
        P("tp", "fsdp"),
        P(None, "tp"),
        P("tp"),
        P(),
        P(),
        P(),
    )
    return jax.shard_map(
        per_device,
        mesh=mesh,
        in_specs=placed,
        out_specs=(
            P("fsdp", "ctx", None),
            P("fsdp", "ctx", None),
            P(None, ("fsdp", "ctx"), "tp"),
            P("tp", ("fsdp", "ctx")),
            P(("fsdp", "ctx"), "tp"),
            P("tp", ("fsdp", "ctx")),
            P(None, "tp", ("fsdp", "ctx")),
            P("tp", ("fsdp", "ctx")),
            P(None, ("fsdp", "ctx")),
            P(None, ("fsdp", "ctx")),
            P(None, ("fsdp", "ctx")),
        ),
        check_vma=False,
    )
```

profile of v0, /device:TPU:0, one launch (start us, length us, event | category | flops | bytes accessed | tf_op | source)
XLA Modules:
  0.0 1568.0 jit_solution(12945536964550515898)
XLA Ops:
  13.4 45.5 %all-gather.7.cloned.1.call-done = bf16[3,768,384]{2,1,0:T(8,128)(2,1)} async-done(((bf16[3,96,384]{2,1,0:T(8,128)(2,1)}), bf16[3,768,384]{2,1,0:T(8,128)(2,1)}) %all-gather.7.cloned.1.call-update) | async-done | bytes 1769488 | tf_op jit(solution)/shard_map/all_gather | solution.py:72
  58.9 3.9 convolution_bitcast_fusion
  69.6 33.5 %all_gather.27 = bf16[384,768]{0,1:T(8,128)(2,1)} all-gather(bf16[384,96]{0,1:T(8,128)(2,1)S(1)} %copy-done.23), channel_id=1, replica_groups=mesh['fsdp'=8,'ctx'=2,'tp'=2] {'fsdp'}, dimensions={1}, use_global_device_ids=true | all-gather | bytes 663552 | tf_op jit(solution)/shard_map/all_gather | solution.py:73
  109.9 14.6 while.39
  113.8 3.3 select_reduce_fusion.2
  121.1 3.3 select_reduce_fusion.2
  124.5 10.1 all-gather.9.cloned.1.call-done
  136.0 20.0 %while.40 = (s32[]{:T(128)}, f32[6,1024,64]{1,2,0:T(8,128)}, s32[]{:T(128)}, s32[2048]{0:T(1024)S(1)}, s32[2048]{0:T(1024)S(1)}, /*index=5*/s32[1024]{0:T(1024)S...) while((s32[]{:T(128)}, f32[6,1024,64]{1,2,0:T(8,128)}, ...), condition=%wide.region_11.12_spmd.clone, body=%wide.region_10.11_spmd.clone.sunk | while | flops 823002112 | bytes 7389387 | solution.py:135
  138.8 7.3 fusion.149
  148.7 7.3 fusion.149
  158.4 3.2 convolution_convert_fusion
  164.0 41.5 %all-reduce.10.cloned.1.call-done = bf16[1024,768]{1,0:T(8,128)(2,1)} async-done(((bf16[1024,768]{1,0:T(8,128)(2,1)}), bf16[1024,768]{1,0:T(8,128)(2,1)}) %all-reduce.10.cloned.1.call-update) | async-done | bytes 1572880 | tf_op jit(solution)/shard_map/psum | solution.py:141
  208.6 52.5 %all-gather.11.cloned.1.call-done = bf16[768,1536]{1,0:T(8,128)(2,1)} async-done(((bf16[96,1536]{1,0:T(8,128)(2,1)}), bf16[768,1536]{1,0:T(8,128)(2,1)}) %all-gather.11.cloned.1.call-update) | async-done | bytes 2359312 | tf_op jit(solution)/shard_map/all_gather | solution.py:74
  261.1 7.7 fusion.82
  268.7 45.2 %all-gather.13.cloned.1.call-done = bf16[1536,768]{0,1:T(8,128)(2,1)} async-done(((bf16[1536,96]{0,1:T(8,128)(2,1)}), bf16[1536,768]{0,1:T(8,128)(2,1)}) %all-gather.13.cloned.1.call-update) | async-done | bytes 2359312 | tf_op jit(solution)/shard_map/all_gather | solution.py:75
  314.0 10.0 convert_reduce_fusion
  325.7 3.7 convolution_convert_fusion.1
  329.5 19.0 %all-reduce.12.cloned.1.call-done = bf16[1024,768]{1,0:T(8,128)(2,1)} async-done(((bf16[1024,768]{1,0:T(8,128)(2,1)}), bf16[1024,768]{1,0:T(8,128)(2,1)}) %all-reduce.12.cloned.1.call-update) | async-done | bytes 1572880 | tf_op jit(solution)/shard_map/psum | solution.py:162
  348.5 4.3 fusion.65
  352.8 3.9 convert_reduce_fusion.5
  363.6 68.0 %while.41 = (s32[]{:T(128)}, f32[6,1024,64]{1,2,0:T(8,128)}, bf16[2048,384]{1,0:T(8,128)(2,1)}, bf16[2048,384]{1,0:T(8,128)(2,1)}, s32[]{:T(128)}, /*index=5*/s3...) while((s32[]{:T(128)}, f32[6,1024,64]{1,2,0:T(8,128)}, ...), condition=%wide.region_20.21_spmd.clone, body=%wide.region_19.20_spmd.clone.sunk | while | flops 2053374976 | bytes 115310968 | solution.py:207
  370.0 3.0 fusion.160
  373.0 5.2 fusion.162
  378.2 7.5 fusion.161
  387.0 5.9 convolution_multiply_fusion.2
  403.6 3.0 fusion.160
  406.6 5.2 fusion.162
  411.8 7.5 fusion.161
  420.6 5.9 convolution_multiply_fusion.2
  432.7 8.8 convolution_convert_fusion.2
  442.0 84.3 %reduce-scatter.18.cloned.1.call-done = bf16[1024,384]{1,0:T(8,128)(2,1)} async-done(((bf16[2048,384]{1,0:T(8,128)(2,1)}), bf16[1024,384]{1,0:T(8,128)(2,1)}) %reduce-scatter.18.cloned.1.call-update) | async-done | bytes 786448 | tf_op jit(solution)/shard_map/reduce_scatter | solution.py:217
  526.3 28.4 %reduce-scatter.16.cloned.1.call-done = bf16[1024,384]{1,0:T(8,128)(2,1)} async-done(((bf16[2048,384]{1,0:T(8,128)(2,1)}), bf16[1024,384]{1,0:T(8,128)(2,1)}) %reduce-scatter.16.cloned.1.call-update) | async-done | bytes 786448 | tf_op jit(solution)/shard_map/reduce_scatter | solution.py:214
  554.8 5.3 bitcast_convert_fusion
  561.9 21.7 %all-reduce.16.cloned.1.call-done = (bf16[1024,768]{1,0:T(8,128)(2,1)}, bf16[1024,768]{1,0:T(8,128)(2,1)}) async-done(((bf16[1024,768]{1,0:T(8,128)(2,1)}, bf16[1024,768]{1,0:T(8,128)(2,1)}), (bf16[1024,768]{1,0:T(8,128)(2,1)}, bf16[1024,768]{1,0:T(8,128)(2,1)})) %all-reduce.16.cloned.1.call-update) | async-done | bytes 3145744 | tf_op jit(solution)/shard_map/psum | solution.py:150
  588.7 5.4 convolution_bitcast_fusion.1
  594.1 6.3 copy.75
  601.6 4.0 fusion.76
  605.9 9.0 fusion.72
  616.3 7.0 fusion.81
  627.8 84.0 %reduce-scatter.26.cloned.1.call-done = f32[48,2]{1,0:T(8,128)} async-done(((f32[768,2]{1,0:T(8,128)}), f32[48,2]{1,0:T(8,128)}) %reduce-scatter.26.cloned.1.call-update) | async-done | bytes 400
  714.5 75.0 %all-reduce.3 = (f32[2,384]{1,0:T(2,128)S(1)}, f32[1536]{0:T(1024)S(1)}) all-reduce(f32[2,384]{1,0:T(2,128)S(1)} %pad_maximum_fusion.6, f32[1536]{0:T(1024)S(1)} %copy-done.41), channel_id=9, replica_groups=mesh['fsdp'=8,'ctx'=2,'tp'=2] {'fsdp','ctx'}, use_global_device_ids=true, to_apply=%region_32.33.clone | all-reduce | flops 2304 | bytes 18432
  790.7 5.4 fusion.57
  796.1 40.9 %reduce-scatter.30.cloned.1.call-done = f32[48,2]{1,0:T(8,128)} async-done(((f32[768,2]{1,0:T(8,128)}), f32[48,2]{1,0:T(8,128)}) %reduce-scatter.30.cloned.1.call-update) | async-done | bytes 400
  838.4 124.7 %reduce-scatter.28.cloned.1.call-done = f32[48,2]{1,0:T(8,128)} async-done(((f32[768,2]{1,0:T(8,128)}), f32[48,2]{1,0:T(8,128)}) %reduce-scatter.28.cloned.1.call-update) | async-done | bytes 400
  964.5 183.1 %all-reduce.14.cloned.1.call-done = f32[3,768,384]{2,0,1:T(4,128)} async-done(((f32[3,768,384]{2,0,1:T(4,128)}), f32[3,768,384]{2,0,1:T(4,128)}) %all-reduce.14.cloned.1.call-update) | async-done | bytes 3538960
  1149.3 126.9 %reduce-scatter.20.cloned.1.call-done = f32[384,48]{0,1:T(8,128)} async-done(((f32[384,768]{0,1:T(8,128)}), f32[384,48]{0,1:T(8,128)}) %reduce-scatter.20.cloned.1.call-update) | async-done | bytes 73744 | tf_op jit(solution)/shard_map/reduce_scatter | solution.py:248
  1276.2 142.3 %reduce-scatter.24.cloned.1.call-done = f32[1536,48]{0,1:T(8,128)} async-done(((f32[1536,768]{0,1:T(8,128)}), f32[1536,48]{0,1:T(8,128)}) %reduce-scatter.24.cloned.1.call-update) | async-done | bytes 294928 | tf_op jit(solution)/shard_map/reduce_scatter | solution.py:250
  1418.5 142.5 %reduce-scatter.22.cloned.1.call-done = f32[48,1536]{1,0:T(8,128)} async-done(((f32[768,1536]{1,0:T(8,128)}), f32[48,1536]{1,0:T(8,128)}) %reduce-scatter.22.cloned.1.call-update) | async-done | bytes 294928 | tf_op jit(solution)/shard_map/reduce_scatter | solution.py:249
  (270 shorter events, 89.8 us)
Async XLA Ops:
  7.2 51.7 %copy-start.4 = (bf16[1,1024,768]{2,1,0:T(8,128)(2,1)S(1)}, bf16[1,1024,768]{2,1,0:T(8,128)(2,1)}, u32[]{:S(2)}) copy-start(bf16[1,1024,768]{2,1,0:T(8,128)(2,1)} %param.18) | copy-start | bytes 4718596
  7.2 51.7 %all-gather.7.cloned.1.call-start = ((), (), s32[]{:S(2)}) async-start(), calls=%async_computation.8 | async-start | bytes 1990656 | tf_op jit(solution)/shard_map/all_gather | solution.py:72
  7.9 101.9 %all-gather.15.cloned.1.call-start = ((), (), s32[]{:S(2)}) async-start(), calls=%async_computation.19 | async-start | bytes 2359296 | tf_op jit(solution)/shard_map/all_gather | solution.py:85
  9.6 53.2 %copy-start.28 = (f32[768]{0:T(1024)}, f32[768]{0:T(1024)S(1)}, u32[]{:S(2)}) copy-start(f32[768]{0:T(1024)S(1)} %get-tuple-element.476) | copy-start | bytes 9220
  9.6 53.2 %copy-start.45 = (f32[768]{0:T(1024)}, f32[768]{0:T(1024)S(1)}, u32[]{:S(2)}) copy-start(f32[768]{0:T(1024)S(1)} %get-tuple-element.382) | copy-start | bytes 9220
  9.6 251.5 %copy-start.43 = (f32[768]{0:T(1024)}, f32[768]{0:T(1024)S(1)}, u32[]{:S(2)}) copy-start(f32[768]{0:T(1024)S(1)} %get-tuple-element.383) | copy-start | bytes 9220
  9.6 343.1 %copy-start.30 = (f32[768]{0:T(1024)}, f32[768]{0:T(1024)S(1)}, u32[]{:S(2)}) copy-start(f32[768]{0:T(1024)S(1)} %get-tuple-element.475) | copy-start | bytes 9220
  11.3 51.5 %copy-start.24 = (f32[1024]{0:T(1024)}, f32[1024]{0:T(1024)S(1)}, u32[]{:S(2)}) copy-start(f32[1024]{0:T(1024)S(1)} %broadcast_multiply_fusion.5) | copy-start | bytes 12292
  13.4 49.5 %copy-start.32 = (f32[1024]{0:T(1024)}, f32[1024]{0:T(1024)S(1)}, u32[]{:S(2)}) copy-start(f32[1024]{0:T(1024)S(1)} %add_rsqrt_fusion.1) | copy-start | bytes 12292
  58.9 7.2 copy-start.50
  58.9 10.6 copy-start.47
  58.9 10.7 copy-start.23
  66.0 68.6 %all-gather.9.cloned.1.call-start = ((), (), s32[]{:S(2)}) async-start(), calls=%async_computation.9 | async-start | bytes 2359296 | tf_op jit(solution)/shard_map/all_gather | solution.py:86
  108.2 97.3 %all-reduce.10.cloned.1.call-start = ((), (), s32[]{:S(2)}) async-start(), calls=%async_computation.10 | async-start | bytes 3145728 | tf_op jit(solution)/shard_map/psum | solution.py:141
  157.5 5.9 copy-start.42
  161.7 99.4 %all-gather.11.cloned.1.call-start = ((), (), s32[]{:S(2)}) async-start(), calls=%async_computation.11 | async-start | bytes 2654208 | tf_op jit(solution)/shard_map/all_gather | solution.py:74
  162.3 151.7 %all-gather.13.cloned.1.call-start = ((), (), s32[]{:S(2)}) async-start(), calls=%async_computation.12 | async-start | bytes 2654208 | tf_op jit(solution)/shard_map/all_gather | solution.py:75
  162.8 185.7 %all-reduce.12.cloned.1.call-start = ((), (), s32[]{:S(2)}) async-start(), calls=%async_computation.13 | async-start | bytes 3145728 | tf_op jit(solution)/shard_map/psum | solution.py:162
  164.0 188.8 %copy-start.21 = (f32[768]{0:T(1024)}, f32[768]{0:T(1024)S(1)}, u32[]{:S(2)}) copy-start(f32[768]{0:T(1024)S(1)} %get-tuple-element.379) | copy-start | bytes 9220
  207.7 145.1 %copy-start.26 = (f32[1024]{0:T(1024)}, f32[1024]{0:T(1024)S(1)}, u32[]{:S(2)}) copy-start(f32[1024]{0:T(1024)S(1)} %broadcast_multiply_fusion.4) | copy-start | bytes 12292
  208.6 144.2 %copy-start.34 = (f32[1024]{0:T(1024)}, f32[1024]{0:T(1024)S(1)}, u32[]{:S(2)}) copy-start(f32[1024]{0:T(1024)S(1)} %add_rsqrt_fusion) | copy-start | bytes 12292
  261.1 52.9 %copy-start.49 = (f32[1536]{0:T(1024)S(1)}, f32[1536]{0:T(1024)}, u32[]{:S(2)}) copy-start(f32[1536]{0:T(1024)} %param.26) | copy-start | bytes 18436
  314.0 11.7 copy-start.48
  329.4 196.9 %reduce-scatter.18.cloned.1.call-start = ((), (), s32[]{:S(2)}) async-start(), calls=%async_computation.15 | async-start | bytes 2359296 | tf_op jit(solution)/shard_map/reduce_scatter | solution.py:217
  352.8 5.6 copy-start.19
  385.7 7.2 copy-start.1
  387.0 5.9 copy-start
  419.3 7.2 copy-start.1
  420.6 5.9 copy-start
  431.7 123.1 %reduce-scatter.16.cloned.1.call-start = ((), (), s32[]{:S(2)}) async-start(), calls=%async_computation.14 | async-start | bytes 2359296 | tf_op jit(solution)/shard_map/reduce_scatter | solution.py:214
  432.4 9.0 copy-start.3
  432.4 151.2 %all-reduce.16.cloned.1.call-start = ((), (), s32[]{:S(2)}) async-start(), calls=%async_computation.24 | async-start | bytes 6291456 | tf_op jit(solution)/shard_map/psum | solution.py:150
  441.6 118.5 %copy-start.13 = (bf16[6,1024,64]{1,2,0:T(8,128)(2,1)}, bf16[6,1024,64]{1,2,0:T(8,128)(2,1)S(1)}, u32[]{:S(2)}) copy-start(bf16[6,1024,64]{1,2,0:T(8,128)(2,1)S(1)} %multiply_convert_fusion.1) | copy-start | bytes 2359300
  560.1 23.5 %copy-start.5 = (bf16[1,1024,768]{2,1,0:T(8,128)(2,1)S(1)}, bf16[1,1024,768]{2,1,0:T(8,128)(2,1)}, u32[]{:S(2)}) copy-start(bf16[1,1024,768]{2,1,0:T(8,128)(2,1)} %param.18) | copy-start | bytes 4718596
  560.1 23.5 %copy-start.25 = (f32[1024]{0:T(1024)S(1)}, f32[1024]{0:T(1024)}, u32[]{:S(2)}) copy-start(f32[1024]{0:T(1024)} %copy-done.24) | copy-start | bytes 12292
  560.2 23.5 %copy-start.29 = (f32[768]{0:T(1024)S(1)}, f32[768]{0:T(1024)}, u32[]{:S(2)}) copy-start(f32[768]{0:T(1024)} %copy-done.28) | copy-start | bytes 9220
  560.2 23.5 %copy-start.33 = (f32[1024]{0:T(1024)S(1)}, f32[1024]{0:T(1024)}, u32[]{:S(2)}) copy-start(f32[1024]{0:T(1024)} %copy-done.32) | copy-start | bytes 12292
  560.2 28.5 %copy-start.20 = (bf16[1024,384]{1,0:T(8,128)(2,1)S(1)}, bf16[1024,384]{1,0:T(8,128)(2,1)}, u32[]{:S(2)}) copy-start(bf16[1024,384]{1,0:T(8,128)(2,1)} %reduce-scatter.18.cloned.1.call-done) | copy-start | bytes 2359300
  560.2 28.5 %copy-start.46 = (f32[768]{0:T(1024)S(1)}, f32[768]{0:T(1024)}, u32[]{:S(2)}) copy-start(f32[768]{0:T(1024)} %copy-done.45) | copy-start | bytes 9220
  560.2 151.6 %reduce-scatter.26.cloned.1.call-start = ((), (), s32[]{:S(2)}) async-start(), calls=%async_computation.20 | async-start | bytes 417792
  561.8 275.2 %reduce-scatter.30.cloned.1.call-start = ((), (), s32[]{:S(2)}) async-start(), calls=%async_computation.22 | async-start | bytes 417792
  587.6 375.6 %reduce-scatter.28.cloned.1.call-start = ((), (), s32[]{:S(2)}) async-start(), calls=%async_computation.21 | async-start | bytes 417792
  588.6 559.0 %all-reduce.14.cloned.1.call-start = ((), (), s32[]{:S(2)}) async-start(), calls=%async_computation.23 | async-start | bytes 9437184
  600.5 675.7 %reduce-scatter.20.cloned.1.call-start = ((), (), s32[]{:S(2)}) async-start(), calls=%async_computation.16 | async-start | bytes 1253376 | tf_op jit(solution)/shard_map/reduce_scatter | solution.py:248
  605.6 812.8 %reduce-scatter.24.cloned.1.call-start = ((), (), s32[]{:S(2)}) async-start(), calls=%async_computation.18 | async-start | bytes 5013504 | tf_op jit(solution)/shard_map/reduce_scatter | solution.py:250
  615.0 946.0 %reduce-scatter.22.cloned.1.call-start = ((), (), s32[]{:S(2)}) async-start(), calls=%async_computation.17 | async-start | bytes 5013504 | tf_op jit(solution)/shard_map/reduce_scatter | solution.py:249
  623.3 91.2 %copy-start.41 = (f32[1536]{0:T(1024)S(1)}, f32[1536]{0:T(1024)}, u32[]{:S(2)}) copy-start(f32[1536]{0:T(1024)} %get-tuple-element.473) | copy-start | bytes 18436
  623.3 167.4 %copy-start.36 = (f32[768]{0:T(1024)S(1)}, f32[768]{0:T(1024)}, u32[]{:S(2)}) copy-start(f32[768]{0:T(1024)} %get-tuple-element.378) | copy-start | bytes 9220
  (27 other events, 58.5 us)
Sparse Core Ops, SparseCore 0:
  10.2 48.6 all-gather.6
  66.1 26.2 all-gather.14
  108.4 26.1 all-gather.8
  161.8 43.6 all-reduce.9
  207.8 53.2 all-gather.10
  263.3 50.6 all-gather.12
  329.5 18.9 all-reduce.11
  431.8 94.4 reduce-scatter.17
  528.6 26.0 reduce-scatter.15
  560.3 23.2 all-reduce.15
  589.0 122.7 reduce-scatter.25
  716.3 120.6 reduce-scatter.29
  842.4 120.7 reduce-scatter.27
  968.7 178.8 all-reduce.13
  1153.5 122.6 reduce-scatter.19
  1282.6 135.8 reduce-scatter.23
  1424.1 136.8 reduce-scatter.21
where the time goes:
time: 1580 us; the launch traced here: 1570 us
  waiting for transfers between devices  1200 us (76%)
  matrix products  134 us (8%)
  blocking collectives  108 us (7%)
  local copies, waits for them, and re-layouts  58.5 us (4%)
  other arithmetic  45.4 us (3%)
  between operations  18.3 us (1%)
    unnamed x21, waiting for transfers between devices  435 us
    reduce_scatter x1, waiting for transfers between devices, per_device(): lax.psum_scatter(up_term, ('fsdp', 'ctx'), scatter_dimension=0, tiled=True)  143 us
    reduce_scatter x1, waiting for transfers between devices, per_device(): lax.psum_scatter(down_term, ('fsdp', 'ctx'), scatter_dimension=1, tiled=T...  142 us
    reduce_scatter x1, waiting for transfers between devices, per_device(): lax.psum_scatter(out_term, ('fsdp', 'ctx'), scatter_dimension=1, tiled=True)  127 us
    reduce_scatter x1, waiting for transfers between devices, per_device(): lax.psum_scatter(value_terms.astype(jnp.bfloat16), 'ctx', scatter_dimensi...  84.3 us
    unnamed x1, blocking collectives  75 us
    all_gather x1, waiting for transfers between devices, per_device(): lax.all_gather(w_up, 'fsdp', axis=0, tiled=True)  52.5 us
    all_gather x1, waiting for transfers between devices, per_device(): lax.all_gather(w_qkv, 'fsdp', axis=1, tiled=True)  45.5 us
  transfers between devices with their start and end apart: 17, of which 16 were waited for; matrix products, arithmetic and copies ran while one was open for 7% of the time, Pallas kernels for 0%

commit v1 on v0

--- a/solution.py
+++ b/solution.py
@@ -27,6 +27,57 @@
 
 def gelu_curve(values):
     return jax.nn.gelu(values, approximate=True)
+
+
+def bits_of(axis):
+    size = lax.axis_size(axis)
+    return [(axis, bit) for bit in range(size.bit_length() - 1)]
+
+
+def swap(values, axis, bit):
+    size = lax.axis_size(axis)
+    return lax.ppermute(values, axis, [(i, i ^ (1 << bit)) for i in range(size)])
+
+
+def gather_rows(shard, axis):
+    size = lax.axis_size(axis)
+    here = lax.axis_index(axis)
+    rows = shard.shape[0]
+    held = shard
+    offsets = [0]
+    for _, bit in reversed(bits_of(axis)):
+        held = jnp.concatenate([held, swap(held, axis, bit)], axis=0)
+        offsets = offsets + [offset ^ (1 << bit) for offset in offsets]
+    place = [offsets.index(offset) for offset in range(size)]
+    place = jnp.array(place, jnp.int32)
+    parts = [
+        lax.dynamic_slice_in_dim(held, place[jnp.bitwise_xor(here, i)] * rows, rows, 0)
+        for i in range(size)
+    ]
+    return jnp.concatenate(parts, axis=0)
+
+
+def scatter_rows(terms, order):
+    fsdp_bits, ctx_bits = len(bits_of("fsdp")), len(bits_of("ctx"))
+    count = fsdp_bits + ctx_bits
+    held = terms.reshape((2,) * count + (terms.shape[0] >> count,) + terms.shape[1:])
+    for step, (axis, bit) in enumerate(order):
+        dim = fsdp_bits - 1 - bit if axis == "fsdp" else count - 1 - bit
+        mine = (lax.axis_index(axis) >> bit) & 1
+        send = lax.dynamic_index_in_dim(held, 1 - mine, dim, keepdims=True)
+        keep = lax.dynamic_index_in_dim(held, mine, dim, keepdims=True)
+        held = keep.astype(jnp.float32) + swap(send, axis, bit).astype(jnp.float32)
+        if step < count - 1:
+            held = held.astype(terms.dtype)
+    return held.reshape(held.shape[count:])
+
+
+def pair_sum(partial):
+    sent = partial.astype(jnp.bfloat16)
+    total = sent.astype(jnp.float32)
+    for axis, bit in bits_of("tp"):
+        total = total + swap(total.astype(jnp.bfloat16), axis, bit).astype(jnp.float32)
+    return total
 
 
 def per_device(
@@ -68,23 +119,18 @@
     block_last_doc = all_doc.reshape(block_count, block)[:, block - 1]
     first_block = jnp.sum((block_last_doc < query_doc[0]).astype(jnp.int32))
     end_block = (first_pos + seg_len - 1) // block + 1
-    gathered = (
-        lax.all_gather(w_qkv, "fsdp", axis=1, tiled=True),
-        lax.all_gather(w_out, "fsdp", axis=1, tiled=True),
-        lax.all_gather(w_up, "fsdp", axis=0, tiled=True),
-        lax.all_gather(w_down, "fsdp", axis=1, tiled=True),
-    )
-    qkv_full, out_full, up_full, down_full = gathered
+    qkv_rows = gather_rows(w_qkv.transpose(1, 0, 2), "fsdp")
+    out_rows = gather_rows(w_out.T, "fsdp")
+    up_full = gather_rows(w_up, "fsdp")
+    down_rows = gather_rows(w_down.T, "fsdp")
     normed, inv_std = normalize(stream)
     hidden = (normed * gains[0] + shifts[0]).astype(jnp.bfloat16)
-    projected = jnp.einsum("td,cde->cte", hidden, qkv_full, preferred_element_type=jnp.float32)
+    projected = jnp.einsum("td,dce->cte", hidden, qkv_rows, preferred_element_type=jnp.float32)
     queries = (projected[0] + qv_bias[0]).astype(jnp.bfloat16)
     keys_local = projected[1].astype(jnp.bfloat16)
     values_local = (projected[2] + qv_bias[1]).astype(jnp.bfloat16)
-    all_keys, all_values = (
-        lax.all_gather(keys_local, "ctx", axis=0, tiled=True),
-        lax.all_gather(values_local, "ctx", axis=0, tiled=True),
-    )
+    all_pairs = gather_rows(jnp.concatenate([keys_local, values_local], axis=1), "ctx")
+    all_keys, all_values = all_pairs[:, :local_width], all_pairs[:, local_width:]
     query_heads = queries.reshape(seg_len, heads_dev, HD)
 
     def take_block(source, block_id):
@@ -136,46 +182,36 @@
         first_block, end_block, mix_step, jnp.zeros((heads_dev, seg_len, HD), jnp.float32)
     )
     mixed = mixed_total.transpose(1, 0, 2).reshape(seg_len, local_width).astype(jnp.bfloat16)
-    partial_attn = jnp.dot(mixed, out_full, preferred_element_type=jnp.float32)
+    partial_attn = jnp.einsum("tc,ec->te", mixed, out_rows, preferred_element_type=jnp.float32)
     middle = (
-        stream + lax.psum(partial_attn.astype(jnp.bfloat16), "tp").astype(jnp.float32) + out_bias[0]
+        stream + pair_sum(partial_attn) + out_bias[0]
     )
     normed_two, inv_two = normalize(middle)
     hidden_two = (normed_two * gains[1] + shifts[1]).astype(jnp.bfloat16)
     pre_act = jnp.dot(hidden_two, up_full, preferred_element_type=jnp.float32) + up_bias
     activ_exact, gelu_pull = jax.vjp(gelu_curve, pre_act)
     activ = activ_exact.astype(jnp.bfloat16)
-    partial_ff = jnp.dot(activ, down_full, preferred_element_type=jnp.float32)
+    partial_ff = jnp.einsum("tf,ef->te", activ, down_rows, preferred_element_type=jnp.float32)
     output = (
-        middle + lax.psum(partial_ff.astype(jnp.bfloat16), "tp").astype(jnp.float32) + out_bias[1]
-    )
-    qkv_back, out_back, up_back, down_back = (
-        lax.all_gather(w_qkv, "fsdp", axis=1, tiled=True),
-        lax.all_gather(w_out, "fsdp", axis=1, tiled=True),
-        lax.all_gather(w_up, "fsdp", axis=0, tiled=True),
-        lax.all_gather(w_down, "fsdp", axis=1, tiled=True),
+        middle + pair_sum(partial_ff) + out_bias[1]
     )
     down_in = grad_out.astype(jnp.bfloat16)
-    act_grad = jnp.einsum("te,fe->tf", down_in, down_back, preferred_element_type=jnp.float32)
+    act_grad = jnp.einsum("te,ef->tf", down_in, down_rows, preferred_element_type=jnp.float32)
     pre_grad = gelu_pull(act_grad)[0].astype(jnp.bfloat16)
-    partial_two = jnp.einsum("tf,df->td", pre_grad, up_back, preferred_element_type=jnp.float32)
-    hidden_two_grad = lax.psum(partial_two.astype(jnp.bfloat16), "tp").astype(jnp.float32)
+    partial_two = jnp.einsum("tf,df->td", pre_grad, up_full, preferred_element_type=jnp.float32)
+    hidden_two_grad = pair_sum(partial_two)
     middle_grad = grad_out + norm_back(hidden_two_grad * gains[1], normed_two, inv_two)
     attn_in = middle_grad.astype(jnp.bfloat16)
     mixed_grad = jnp.einsum(
-        "te,ce->tc", attn_in, out_back, preferred_element_type=jnp.float32
+        "te,ec->tc", attn_in, out_rows, preferred_element_type=jnp.float32
     ).astype(jnp.bfloat16)
     grad_heads = mixed_grad.reshape(seg_len, heads_dev, HD)
-    back_keys, back_values = (
-        lax.all_gather(keys_local, "ctx", axis=0, tiled=True),
-        lax.all_gather(values_local, "ctx", axis=0, tiled=True),
-    )
     delta = jnp.einsum("qhd,hqd->hq", grad_heads.astype(jnp.float32), mixed_total)
 
     def grad_step(block_id, carry):
         query_total, key_buffer, value_buffer = carry
-        key_part = take_block(back_keys, block_id)
-        value_part = take_block(back_values, block_id)
+        key_part = take_block(all_keys, block_id)
+        value_part = take_block(all_values, block_id)
         scores, allowed = block_scores(key_part, block_id)
         weights = probs_of(scores, allowed)
         weight_grad = jnp.einsum(
@@ -210,29 +246,31 @@
         grad_step,
         (jnp.zeros((heads_dev, seg_len, HD), jnp.float32), empty_row, empty_row),
     )
-    key_grad, value_grad = (
-        lax.psum_scatter(
-            key_terms.astype(jnp.bfloat16), "ctx", scatter_dimension=0, tiled=True
-        ).astype(jnp.float32),
-        lax.psum_scatter(
-            value_terms.astype(jnp.bfloat16), "ctx", scatter_dimension=0, tiled=True
-        ).astype(jnp.float32),
-    )
+    pair_terms = jnp.concatenate([key_terms, value_terms], axis=1).astype(jnp.bfloat16)
+    pair_grad = pair_terms.reshape(ctx_count, seg_len, 2 * local_width)
+    for axis, bit in reversed(bits_of("ctx")):
+        split = pair_grad.reshape((2, pair_grad.shape[0] // 2) + pair_grad.shape[1:])
+        mine = (ctx_here >> bit) & 1
+        send = lax.dynamic_index_in_dim(split, 1 - mine, 0, keepdims=False)
+        keep = lax.dynamic_index_in_dim(split, mine, 0, keepdims=False)
+        pair_grad = keep.astype(jnp.float32) + swap(send, axis, bit).astype(jnp.float32)
+        pair_grad = pair_grad.astype(jnp.bfloat16)
+    key_grad, value_grad = pair_grad[0][:, :local_width], pair_grad[0][:, local_width:]
     query_grad = query_total.transpose(1, 0, 2).reshape(seg_len, local_width) * scale
-    qkv_grad_in = jnp.stack([query_grad, key_grad, value_grad]).astype(jnp.bfloat16)
+    qkv_grad_in = jnp.stack([query_grad.astype(jnp.bfloat16), key_grad, value_grad], axis=1)
     partial_hidden = jnp.einsum(
-        "cte,cde->td", qkv_grad_in, qkv_back, preferred_element_type=jnp.float32
-    )
-    hidden_grad = lax.psum(partial_hidden.astype(jnp.bfloat16), "tp").astype(jnp.float32)
+        "tce,dce->td", qkv_grad_in, qkv_rows, preferred_element_type=jnp.float32
+    )
+    hidden_grad = pair_sum(partial_hidden)
     token_grad = middle_grad + norm_back(hidden_grad * gains[0], normed, inv_std)
-    qkv_term = jnp.einsum("td,cte->cde", hidden, qkv_grad_in, preferred_element_type=jnp.float32)
-    out_term = jnp.einsum("tc,te->ce", mixed, attn_in, preferred_element_type=jnp.float32)
+    qkv_term = jnp.einsum("td,tce->dce", hidden, qkv_grad_in, preferred_element_type=jnp.float32)
+    out_term = jnp.einsum("te,tc->ec", attn_in, mixed, preferred_element_type=jnp.float32)
     up_term = jnp.einsum("td,tf->df", hidden_two, pre_grad, preferred_element_type=jnp.float32)
-    down_term = jnp.einsum("tf,te->fe", activ, down_in, preferred_element_type=jnp.float32)
+    down_term = jnp.einsum("te,tf->ef", down_in, activ, preferred_element_type=jnp.float32)
     qv_term = jnp.stack(
         [
-            jnp.sum(qkv_grad_in[0].astype(jnp.float32), axis=0),
-            jnp.sum(qkv_grad_in[2].astype(jnp.float32), axis=0),
+            jnp.sum(qkv_grad_in[:, 0].astype(jnp.float32), axis=0),
+            jnp.sum(qkv_grad_in[:, 2].astype(jnp.float32), axis=0),
         ]
     )
     up_bias_term = jnp.sum(pre_grad.astype(jnp.float32), axis=0)
@@ -243,29 +281,43 @@
         [jnp.sum(hidden_grad * normed, axis=0), jnp.sum(hidden_two_grad * normed_two, axis=0)]
     )
     shifts_term = jnp.stack([jnp.sum(hidden_grad, axis=0), jnp.sum(hidden_two_grad, axis=0)])
-    summed = (
-        lax.psum_scatter(qkv_term, ("fsdp", "ctx"), scatter_dimension=1, tiled=True),
-        lax.psum_scatter(out_term, ("fsdp", "ctx"), scatter_dimension=1, tiled=True),
-        lax.psum_scatter(up_term, ("fsdp", "ctx"), scatter_dimension=0, tiled=True),
-        lax.psum_scatter(down_term, ("fsdp", "ctx"), scatter_dimension=1, tiled=True),
-        lax.psum_scatter(qv_term, ("fsdp", "ctx"), scatter_dimension=1, tiled=True),
-        lax.psum_scatter(up_bias_term, ("fsdp", "ctx"), scatter_dimension=0, tiled=True),
-        lax.psum_scatter(out_bias_term, ("fsdp", "ctx"), scatter_dimension=1, tiled=True),
-        lax.psum_scatter(gains_term, ("fsdp", "ctx"), scatter_dimension=1, tiled=True),
-        lax.psum_scatter(shifts_term, ("fsdp", "ctx"), scatter_dimension=1, tiled=True),
-    )
+    along_ctx, along_fsdp = bits_of("ctx"), bits_of("fsdp")
+    ctx_first = along_ctx + along_fsdp
+    fsdp_first = along_fsdp[:1] + along_ctx + along_fsdp[1:]
+    parts = lax.axis_size("fsdp") * ctx_count
+    down_sum = scatter_rows(down_term.astype(jnp.bfloat16), ctx_first)
+    up_sum = scatter_rows(up_term.astype(jnp.bfloat16), fsdp_first)
+    out_sum = scatter_rows(out_term.astype(jnp.bfloat16), ctx_first)
+    qkv_sum = scatter_rows(
+        qkv_term.astype(jnp.bfloat16).reshape(qkv_term.shape[0], 3 * local_width), ctx_first
+    )
+
+    def in_parts(term):
+        lead = term.shape[0]
+        return term.reshape(lead, parts, -1).transpose(1, 0, 2).reshape(parts, -1)
+
+    small = [qv_term, up_bias_term[None], out_bias_term, gains_term, shifts_term]
+    small_sum = scatter_rows(
+        jnp.concatenate([in_parts(term) for term in small], axis=1), ctx_first
+    ).reshape(-1)
+    small_sums = []
+    start = 0
+    for term in small:
+        size = term.size // parts
+        small_sums.append(small_sum[start : start + size].reshape(term.shape[0], -1))
+        start += size
     return (
         output[None],
         token_grad[None],
-        summed[0],
-        summed[1],
-        summed[2],
-        summed[3],
-        summed[4][:, None, :],
-        summed[5][None, :],
-        summed[6],
-        summed[7],
-        summed[8],
+        qkv_sum.reshape(-1, 3, local_width).transpose(1, 0, 2),
+        out_sum.T,
+        up_sum,
+        down_sum.T,
+        small_sums[0][:, None, :],
+        small_sums[1],
+        small_sums[2],
+        small_sums[3],
+        small_sums[4],
     )
 
 

time: 1580 us -> 557 us (0.35)
  waiting for transfers between devices: 1200 us -> 115 us
  starting transfers between devices: 1.68 us -> 149 us
  blocking collectives: 108 us -> 0 us
  local copies, waits for them, and re-layouts: 58.5 us -> 101 us
  matrix products: 134 us -> 94.1 us
  other arithmetic: 45.4 us -> 71.2 us
    reduce_scatter x5 -> x0, waiting for transfers between devices: 524 us -> none  [the longest x1 143 us: per_device(): lax.psum_scatter(up_term, ('fsdp', 'ctx'), scatter_dimension=0, tiled=True)]
    unnamed x21 -> x0, waiting for transfers between devices: 435 us -> none
    all_gather x5 -> x0, waiting for transfers between devices: 153 us -> none  [the longest x1 52.5 us: per_device(): lax.all_gather(w_up, 'fsdp', axis=0, tiled=True)]
    ppermute x0 -> x38, starting transfers between devices: none -> 149 us  [swap(): return lax.ppermute(values, axis, [(i, i ^ 1 << bit) for i in range(size)])]
    ppermute x0 -> x38, waiting for transfers between devices: none -> 115 us  [swap(): return lax.ppermute(values, axis, [(i, i ^ 1 << bit) for i in range(size)])]
    psum x3 -> x0, waiting for transfers between devices: 82.3 us -> none  [the longest x1 41.5 us: per_device(): lax.psum(partial_attn.astype(jnp.bfloat16), 'tp').astype(jnp.float32)]
    unnamed x1 -> x0, blocking collectives: 75 us -> none
    all_gather x1 -> x0, blocking collectives: 33.5 us -> none  [per_device(): lax.all_gather(w_out, 'fsdp', axis=1, tiled=True)]
  transfers between devices with their start and end apart: 17 -> 38, of which waited for: 16 -> 17; matrix products, arithmetic and copies ran while one was open for 7% -> 34% of each run, Pallas kernels for 0% -> 0%
where the time goes in v1:
time: 557 us; the launch traced here: 546 us
  starting transfers between devices  149 us (27%)
  waiting for transfers between devices  115 us (21%)
  local copies, waits for them, and re-layouts  101 us (18%)
  matrix products  94.1 us (17%)
  other arithmetic  71.2 us (13%)
  between operations  8.63 us (2%)
  loops' own time  5.81 us (1%)
    ppermute x38, starting transfers between devices, swap(): return lax.ppermute(values, axis, [(i, i ^ 1 << bit) for i in range(size)])  149 us
    ppermute x38, waiting for transfers between devices, swap(): return lax.ppermute(values, axis, [(i, i ^ 1 << bit) for i in range(size)])  115 us
    unnamed x159, local copies, waits for them, and re-layouts  34.8 us
    concatenate x12, other arithmetic, gather_rows(): held = jnp.concatenate([held, swap(held, axis, bit)], axis=0)  14.7 us
    dot_general x4, matrix products, block_scores(): jnp.einsum('qhd,khd->hqk', query_heads, key_part, preferred_element_type=...  12.5 us
    dot_general x2, matrix products, mix_step(): jnp.einsum('hqk,khd->hqd', weights, value_part, preferred_element_type=jn...  12 us
    dynamic_slice x8, local copies, waits for them, and re-layouts, take_block(): lax.dynamic_slice_in_dim(source, block_id * block, block, 0)  11.5 us
    dot_general x2, matrix products, grad_step(): jnp.einsum('qhd,khd->hqk', grad_heads, value_part, preferred_element_type...  11.5 us
  transfers between devices with their start and end apart: 38, of which 17 were waited for; matrix products, arithmetic and copies ran while one was open for 34% of the time, Pallas kernels for 0%

profile of v1, /device:TPU:0, one launch (start us, length us, event | category | flops | bytes accessed | tf_op | source)
XLA Modules:
  0.0 545.8 jit_solution(306072825131771572)
XLA Ops:
  0.6 4.1 collective-permute-start.4
  18.4 11.1 %collective-permute-start.5 = (bf16[192,384]{1,0:T(8,128)(2,1)}, bf16[192,384]{1,0:T(8,128)(2,1)}, u32[]{:S(2)}, u32[]{:S(2)}) collective-permute-start(bf16[192,384]{1,0:T(8,128)(2,1)} %pad_maximum_fusion.16), channel_id=1, source_target_pairs={{0,8},{4,12},{8,0},{12,4},{16,24},{20,28},{24,16},{28,20},{1,9},{5... | collective-permute-start | bytes 442376 | tf_op jit(solution)/shard_map/ppermute | solution.py:39
  38.4 3.5 copy.125
  42.0 8.2 %collective-permute-done.5 = bf16[192,384]{1,0:T(8,128)(2,1)} collective-permute-done((bf16[192,384]{1,0:T(8,128)(2,1)}, bf16[192,384]{1,0:T(8,128)(2,1)}, u32[]{:S(2)}, u32[]{:S(2)}) %collective-permute-start.5) | collective-permute-done | bytes 147488 | tf_op jit(solution)/shard_map/ppermute | solution.py:39
  63.9 6.1 %collective-permute-done.1 = bf16[192,3,384]{2,0,1:T(8,128)(2,1)} collective-permute-done((bf16[192,3,384]{2,0,1:T(8,128)(2,1)}, bf16[192,3,384]{2,0,1:T(8,128)(2,1)}, u32[]{:S(2)}, u32[]{:S(2)}) %collective-permute-start.1) | collective-permute-done | bytes 442400 | tf_op jit(solution)/shard_map/ppermute | solution.py:39
  74.8 7.8 %collective-permute-done.12 = bf16[192,1536]{1,0:T(8,128)(2,1)} collective-permute-done((bf16[192,1536]{1,0:T(8,128)(2,1)}, bf16[192,1536]{1,0:T(8,128)(2,1)}, u32[]{:S(2)}, u32[]{:S(2)}) %collective-permute-start.12) | collective-permute-done | bytes 589856 | tf_op jit(solution)/shard_map/ppermute | solution.py:39
  85.2 8.7 %collective-permute-done.9 = bf16[192,1536]{1,0:T(8,128)(2,1)} collective-permute-done((bf16[192,1536]{1,0:T(8,128)(2,1)}, bf16[192,1536]{1,0:T(8,128)(2,1)}, u32[]{:S(2)}, u32[]{:S(2)}) %collective-permute-start.9) | collective-permute-done | bytes 589856 | tf_op jit(solution)/shard_map/ppermute | solution.py:39
  101.2 4.1 concatenate.101
  105.3 3.6 convolution_bitcast_fusion
  114.1 6.7 %collective-permute-done.13 = bf16[384,1536]{1,0:T(8,128)(2,1)} collective-permute-done((bf16[384,1536]{1,0:T(8,128)(2,1)}, bf16[384,1536]{1,0:T(8,128)(2,1)}, u32[]{:S(2)}, u32[]{:S(2)}) %collective-permute-start.13) | collective-permute-done | bytes 1179680 | tf_op jit(solution)/shard_map/ppermute | solution.py:39
  122.3 20.2 %collective-permute-done.10 = bf16[384,1536]{1,0:T(8,128)(2,1)} collective-permute-done((bf16[384,1536]{1,0:T(8,128)(2,1)}, bf16[384,1536]{1,0:T(8,128)(2,1)}, u32[]{:S(2)}, u32[]{:S(2)}) %collective-permute-start.10) | collective-permute-done | bytes 1179680 | tf_op jit(solution)/shard_map/ppermute | solution.py:39
  150.2 17.0 %while.39 = (s32[]{:T(128)}, f32[6,1024]{1,0:T(8,128)S(1)}, f32[6,1024]{1,0:T(8,128)S(1)}, s32[]{:T(128)}, s32[2048]{0:T(1024)S(1)}, /*index=5*/s32[2048]{0:T(10...) while((s32[]{:T(128)}, f32[6,1024]{1,0:T(8,128)S(1)}, ...), condition=%wide.region_9.10_spmd.clone, body=%wide.region_6.9_spmd.clone.sunk | while | flops 429405184 | bytes 29049028 | solution.py:165
  152.1 3.3 fusion.153
  155.4 3.3 select_reduce_fusion.2
  160.5 3.3 fusion.153
  163.8 3.3 select_reduce_fusion.2
  168.6 20.2 %while.40 = (s32[]{:T(128)}, f32[6,1024,64]{1,2,0:T(8,128)S(1)}, s32[]{:T(128)}, s32[2048]{0:T(1024)}, s32[2048]{0:T(1024)S(1)}, /*index=5*/s32[1024]{0:T(1024)S...) while((s32[]{:T(128)}, f32[6,1024,64]{1,2,0:T(8,128)S(1)}, ...), condition=%wide.region_11.12_spmd.clone, body=%wide.region_10.11_spmd.clone.sunk | while | flops 823002112 | bytes 7389387 | solution.py:181
  172.7 6.0 %fusion.158 = f32[6,1024,64]{1,2,0:T(8,128)S(1)} fusion(f32[6,1024,64]{1,2,0:T(8,128)S(1)} %get-tuple-element.794, bf16[512,6,64]{0,2,1:T(8,128)(2,1)S(1)} %bitcast.308, f32[6,1024]{1,0:T(8,128)} %get-tuple-element.816, pred[1024,512]{0,1:T(8,128)(4,1)} %compare_and_fusion.7, bf16[512,6,64]{0,2,1:T(8,128)(2,1)} %bitcast.309, ...), kind=kOutput, calls=%fused_computation.19.clone.1 | convolution fusion | flops 821428224 | bytes 5267456 | tf_op jit(solution)/shard_map/while/body/hqk,khd->hqd/dot_general | solution.py:177
  182.9 6.0 %fusion.158 = f32[6,1024,64]{1,2,0:T(8,128)S(1)} fusion(f32[6,1024,64]{1,2,0:T(8,128)S(1)} %get-tuple-element.794, bf16[512,6,64]{0,2,1:T(8,128)(2,1)S(1)} %bitcast.308, f32[6,1024]{1,0:T(8,128)} %get-tuple-element.816, pred[1024,512]{0,1:T(8,128)(4,1)} %compare_and_fusion.7, bf16[512,6,64]{0,2,1:T(8,128)(2,1)} %bitcast.309, ...), kind=kOutput, calls=%fused_computation.19.clone.1 | convolution fusion | flops 821428224 | bytes 5267456 | tf_op jit(solution)/shard_map/while/body/hqk,khd->hqd/dot_general | solution.py:177
  201.5 3.7 convolution_convert_fusion
  205.3 7.0 %convert_reduce_fusion = (f32[1536]{0:T(1024)S(1)}, bf16[1024,1536]{1,0:T(8,128)(2,1)S(1)}) fusion(f32[1024,1536]{1,0:T(8,128)S(1)} %fusion.89, f32[1536]{0:T(1024)S(1)} %copy-done.69, bf16[768,1536]{1,0:T(8,128)(2,1)S(1)} %copy-done.57, f32[1,1024,768]{1,2,0:T(8,128)S(1)} %copy-done.8), kind=kOutput, calls=%fused_computation.60 | convolution fusion | flops 2452093440 | bytes 14954496 | tf_op jit(solution)/shard_map/te,ef->tf/dot_general | solution.py:199
  214.9 3.2 convolution_convert_fusion.1
  222.7 4.1 convolution_convert_fusion.5
  227.5 20.5 %collective-permute-done.30 = bf16[2,2,2,1,48,1536]{5,4,3,2,1,0:T(8,128)(2,1)} collective-permute-done((bf16[2,2,2,1,48,1536]{5,4,3,2,1,0:T(8,128)(2,1)}, bf16[2,2,2,1,48,1536]{5,4,3,2,1,0:T(8,128)(2,1)}, u32[]{:S(2)}, u32[]{:S(2)}) %collective-permute-start.30) | collective-permute-done | bytes 1179680 | tf_op jit(solution)/shard_map/ppermute | solution.py:39
  256.0 3.6 multiply_reduce_fusion
  259.6 5.2 convert_reduce_fusion.3
  272.7 53.8 %while.41 = (s32[]{:T(128)}, f32[6,1024,64]{1,2,0:T(8,128)}, bf16[2048,384]{0,1:T(8,128)(2,1)}, bf16[2048,384]{0,1:T(8,128)(2,1)}, s32[]{:T(128)}, /*index=5*/s3...) while((s32[]{:T(128)}, f32[6,1024,64]{1,2,0:T(8,128)}, ...), condition=%wide.region_17.18_spmd.clone, body=%wide.region_16.17_spmd.clone.sunk | while | flops 2053374976 | bytes 90145144 | solution.py:243
  281.6 5.2 fusion.171
  286.8 5.7 %fusion.170 = bf16[6,1024,512]{1,2,0:T(8,128)(2,1)S(1)} fusion(f32[6,512,1024]{2,1,0:T(8,128)S(1)} %fusion.169, f32[6,1024]{1,0:T(8,128)S(1)} %get-tuple-element.874, f32[6,1024]{1,0:T(8,128)S(1)} %get-tuple-element.871, pred[1024,512]{0,1:T(8,128)(4,1)} %compare_and_fusion.8, bf16[512,6,64]{0,2,1:T(8,128)(2,1)} %bitcast.307, ...), kind=kOutput, calls=%fused_computation.27.clone.1 | convolution fusion | flops 424673280 | bytes 20627456 | tf_op jit(solution)/shard_map/while/body/qhd,khd->hqk/dot_general | solution.py:217
  292.6 3.3 convolution_multiply_fusion.2
  308.1 5.2 fusion.171
  313.3 5.7 %fusion.170 = bf16[6,1024,512]{1,2,0:T(8,128)(2,1)S(1)} fusion(f32[6,512,1024]{2,1,0:T(8,128)S(1)} %fusion.169, f32[6,1024]{1,0:T(8,128)S(1)} %get-tuple-element.874, f32[6,1024]{1,0:T(8,128)S(1)} %get-tuple-element.871, pred[1024,512]{0,1:T(8,128)(4,1)} %compare_and_fusion.8, bf16[512,6,64]{0,2,1:T(8,128)(2,1)} %bitcast.307, ...), kind=kOutput, calls=%fused_computation.27.clone.1 | convolution fusion | flops 424673280 | bytes 20627456 | tf_op jit(solution)/shard_map/while/body/qhd,khd->hqk/dot_general | solution.py:217
  319.1 3.3 convolution_multiply_fusion.2
  340.5 3.5 copy.133
  345.6 89.1 %collective-permute-start.32 = (bf16[2,1,1,1,48,1536]{5,4,3,2,1,0:T(8,128)(2,1)S(1)}, bf16[2,1,1,1,48,1536]{5,4,3,2,1,0:T(8,128)(2,1)S(1)}, u32[]{:S(2)}, u32[]{:S(2)}) collective-permute-start(bf16[2,1,1,1,48,1536]{5,4,3,2,1,0:T(8,128)(2,1)S(1)} %constant_dynamic-slice_fusion.19), channel_id=1, source_target_pairs={{0,8},{4,12},{8,0},{12,4},{16,24},{20,28},{24,16},{28,20},{1,9},{5... | collective-permute-start | bytes 884744 | tf_op jit(solution)/shard_map/ppermute | solution.py:39
  437.5 3.8 collective-permute-done.23
  444.0 7.0 %collective-permute-done.28 = bf16[2,1,1,1,48,1536]{5,4,3,2,1,0:T(8,128)(2,1)S(1)} collective-permute-done((bf16[2,1,1,1,48,1536]{5,4,3,2,1,0:T(8,128)(2,1)S(1)}, bf16[2,1,1,1,48,1536]{5,4,3,2,1,0:T(8,128)(2,1)S(1)}, u32[]{:S(2)}, u32[]{:S(2)}) %collective-permute-start.28) | collective-permute-done | bytes 294944 | tf_op jit(solution)/shard_map/ppermute | solution.py:39
  455.0 3.4 collective-permute-done.25
  469.6 4.3 reshape_reshape.8
  477.9 5.0 bitcast_convert_fusion
  482.9 8.3 %collective-permute-done.18 = bf16[2,2,2,1,48,1152]{5,4,3,2,1,0:T(8,128)(2,1)S(1)} collective-permute-done((bf16[2,2,2,1,48,1152]{5,4,3,2,1,0:T(8,128)(2,1)S(1)}, bf16[2,2,2,1,48,1152]{5,4,3,2,1,0:T(8,128)(2,1)S(1)}, u32[]{:S(2)}, u32[]{:S(2)}) %collective-permute-start.18) | collective-permute-done | bytes 884768 | tf_op jit(solution)/shard_map/ppermute | solution.py:39
  495.0 4.9 collective-permute-done.19
  500.0 9.4 %collective-permute-start.20 = (bf16[2,1,1,1,48,1152]{5,4,3,2,1,0:T(8,128)(2,1)S(1)}, bf16[2,1,1,1,48,1152]{5,4,3,2,1,0:T(8,128)(2,1)S(1)}, u32[]{:S(2)}, u32[]{:S(2)}) collective-permute-start(bf16[2,1,1,1,48,1152]{5,4,3,2,1,0:T(8,128)(2,1)S(1)} %constant_dynamic-slice_fusion.10), channel_id=1, source_target_pairs={{0,8},{4,12},{8,0},{12,4},{16,24},{20,28},{24,16},{28,20},{1,9},{5... | collective-permute-start | bytes 663560 | tf_op jit(solution)/shard_map/ppermute | solution.py:39
  509.8 3.5 collective-permute-done.20
  513.4 3.4 fusion.58
  518.4 3.2 collective-permute-start.21
  531.9 5.9 %fusion.57 = f32[1,1024,768]{1,2,0:T(8,128)} fusion(f32[1024,768]{0,1:T(8,128)} %copy-done.5, bf16[1,1024,768]{1,2,0:T(8,128)(2,1)S(1)} %copy-done.4, bf16[1024,768]{0,1:T(8,128)(2,1)} %collective-permute-done.17, bf16[1024,768]{0,1:T(8,128)(2,1)} %bitcast_convert_fusion, f32[1024]{0:T(1024)S(1)} %broadcast_multiply_fusion, ...), kind=kLoop, calls=%fused_computation.84 | loop fusion | flops 9437184 | bytes 11029504 | tf_op jit(solution)/shard_map/broadcast_in_dim | solution.py:311
  537.8 3.5 copy.134
  (425 shorter events, 187.9 us)
Async XLA Ops:
  0.6 17.1 %collective-permute-start.4 = (bf16[96,384]{1,0:T(8,128)(2,1)}, bf16[96,384]{1,0:T(8,128)(2,1)S(1)}, u32[]{:S(2)}, u32[]{:S(2)}) collective-permute-start(bf16[96,384]{1,0:T(8,128)(2,1)} %bitcast.331), channel_id=1, source_target_pairs={{0,16},{4,20},{8,24},{12,28},{16,0},{20,4},{24,8},{28,12},{1,17},{... | collective-permute-start | bytes 221192 | tf_op jit(solution)/shard_map/ppermute | solution.py:39
  5.9 47.5 %collective-permute-start = (bf16[96,3,384]{0,2,1:T(8,128)(2,1)S(1)}, bf16[96,3,384]{0,2,1:T(8,128)(2,1)S(1)}, u32[]{:S(2)}, u32[]{:S(2)}) collective-permute-start(bf16[96,3,384]{0,2,1:T(8,128)(2,1)S(1)} %bitcast.311), channel_id=1, source_target_pairs={{0,16},{4,20},{8,24},{12,28},{16,0},{20,4},{24,8},{28,12},{1,17},{... | collective-permute-start | bytes 663560 | tf_op jit(solution)/shard_map/ppermute | solution.py:39
  6.0 50.6 %collective-permute-start.11 = (bf16[96,1536]{1,0:T(8,128)(2,1)}, bf16[96,1536]{1,0:T(8,128)(2,1)S(1)}, u32[]{:S(2)}, u32[]{:S(2)}) collective-permute-start(bf16[96,1536]{1,0:T(8,128)(2,1)} %bitcast.320), channel_id=1, source_target_pairs={{0,16},{4,20},{8,24},{12,28},{16,0},{20,4},{24,8},{28,12},{1,17},{... | collective-permute-start | bytes 884744 | tf_op jit(solution)/shard_map/ppermute | solution.py:39
  8.9 50.6 %collective-permute-start.8 = (bf16[96,1536]{1,0:T(8,128)(2,1)}, bf16[96,1536]{1,0:T(8,128)(2,1)S(1)}, u32[]{:S(2)}, u32[]{:S(2)}) collective-permute-start(bf16[96,1536]{1,0:T(8,128)(2,1)} %param.28), channel_id=1, source_target_pairs={{0,16},{4,20},{8,24},{12,28},{16,0},{20,4},{24,8},{28,12},{1,17},{... | collective-permute-start | bytes 884744 | tf_op jit(solution)/shard_map/ppermute | solution.py:39
  14.6 90.7 %copy-start.50 = (f32[768]{0:T(1024)}, f32[768]{0:T(1024)S(1)}, u32[]{:S(2)}) copy-start(f32[768]{0:T(1024)S(1)} %get-tuple-element.381) | copy-start | bytes 9220
  16.3 180.8 %copy-start.3 = (bf16[1,1024,768]{1,2,0:T(8,128)(2,1)}, bf16[1,1024,768]{1,2,0:T(8,128)(2,1)S(1)}, u32[]{:S(2)}) copy-start(bf16[1,1024,768]{1,2,0:T(8,128)(2,1)S(1)} %copy.117) | copy-start | bytes 4718596
  16.6 88.6 %copy-start.48 = (f32[1024]{0:T(1024)}, f32[1024]{0:T(1024)S(1)}, u32[]{:S(2)}) copy-start(f32[1024]{0:T(1024)S(1)} %broadcast_multiply_fusion.5) | copy-start | bytes 12292
  17.1 88.1 %copy-start.52 = (f32[1024]{0:T(1024)}, f32[1024]{0:T(1024)S(1)}, u32[]{:S(2)}) copy-start(f32[1024]{0:T(1024)S(1)} %add_rsqrt_fusion.1) | copy-start | bytes 12292
  17.7 87.5 %copy-start.65 = (f32[768]{0:T(1024)}, f32[768]{0:T(1024)S(1)}, u32[]{:S(2)}) copy-start(f32[768]{0:T(1024)S(1)} %get-tuple-element.383) | copy-start | bytes 9220
  18.4 31.8 %collective-permute-start.5 = (bf16[192,384]{1,0:T(8,128)(2,1)}, bf16[192,384]{1,0:T(8,128)(2,1)}, u32[]{:S(2)}, u32[]{:S(2)}) collective-permute-start(bf16[192,384]{1,0:T(8,128)(2,1)} %pad_maximum_fusion.16), channel_id=1, source_target_pairs={{0,8},{4,12},{8,0},{12,4},{16,24},{20,28},{24,16},{28,20},{1,9},{5... | collective-permute-start | bytes 442376 | tf_op jit(solution)/shard_map/ppermute | solution.py:39
  51.8 9.3 %collective-permute-start.6 = (bf16[384,384]{1,0:T(8,128)(2,1)}, bf16[384,384]{1,0:T(8,128)(2,1)}, u32[]{:S(2)}, u32[]{:S(2)}) collective-permute-start(bf16[384,384]{1,0:T(8,128)(2,1)} %pad_maximum_fusion.15), channel_id=1, source_target_pairs={{0,4},{4,0},{8,12},{12,8},{16,20},{20,16},{24,28},{28,24},{1,5},{5... | collective-permute-start | bytes 884744 | tf_op jit(solution)/shard_map/ppermute | solution.py:39
  56.6 13.4 %collective-permute-start.1 = (bf16[192,3,384]{2,0,1:T(8,128)(2,1)}, bf16[192,3,384]{2,0,1:T(8,128)(2,1)}, u32[]{:S(2)}, u32[]{:S(2)}) collective-permute-start(bf16[192,3,384]{2,0,1:T(8,128)(2,1)} %copy.120), channel_id=1, source_target_pairs={{0,8},{4,12},{8,0},{12,4},{16,24},{20,28},{24,16},{28,20},{1,9},{5... | collective-permute-start | bytes 1327112 | tf_op jit(solution)/shard_map/ppermute | solution.py:39
  57.5 25.1 %collective-permute-start.12 = (bf16[192,1536]{1,0:T(8,128)(2,1)}, bf16[192,1536]{1,0:T(8,128)(2,1)}, u32[]{:S(2)}, u32[]{:S(2)}) collective-permute-start(bf16[192,1536]{1,0:T(8,128)(2,1)} %pad_maximum_fusion.14), channel_id=1, source_target_pairs={{0,8},{4,12},{8,0},{12,4},{16,24},{20,28},{24,16},{28,20},{1,9},{5... | collective-permute-start | bytes 1769480 | tf_op jit(solution)/shard_map/ppermute | solution.py:39
  60.4 33.5 %collective-permute-start.9 = (bf16[192,1536]{1,0:T(8,128)(2,1)}, bf16[192,1536]{1,0:T(8,128)(2,1)}, u32[]{:S(2)}, u32[]{:S(2)}) collective-permute-start(bf16[192,1536]{1,0:T(8,128)(2,1)} %pad_maximum_fusion.13), channel_id=1, source_target_pairs={{0,8},{4,12},{8,0},{12,4},{16,24},{20,28},{24,16},{28,20},{1,9},{5... | collective-permute-start | bytes 1769480 | tf_op jit(solution)/shard_map/ppermute | solution.py:39
  72.7 25.8 %collective-permute-start.2 = (bf16[384,3,384]{0,2,1:T(8,128)(2,1)S(1)}, bf16[384,3,384]{0,2,1:T(8,128)(2,1)S(1)}, u32[]{:S(2)}, u32[]{:S(2)}) collective-permute-start(bf16[384,3,384]{0,2,1:T(8,128)(2,1)S(1)} %pad_maximum_fusion.10), channel_id=1, source_target_pairs={{0,4},{4,0},{8,12},{12,8},{16,20},{20,16},{24,28},{28,24},{1,5},{5... | collective-permute-start | bytes 2654216 | tf_op jit(solution)/shard_map/ppermute | solution.py:39
  84.8 36.0 %collective-permute-start.13 = (bf16[384,1536]{1,0:T(8,128)(2,1)}, bf16[384,1536]{1,0:T(8,128)(2,1)}, u32[]{:S(2)}, u32[]{:S(2)}) collective-permute-start(bf16[384,1536]{1,0:T(8,128)(2,1)} %pad_maximum_fusion.7), channel_id=1, source_target_pairs={{0,4},{4,0},{8,12},{12,8},{16,20},{20,16},{24,28},{28,24},{1,5},{5... | collective-permute-start | bytes 3538952 | tf_op jit(solution)/shard_map/ppermute | solution.py:39
  96.2 46.4 %collective-permute-start.10 = (bf16[384,1536]{1,0:T(8,128)(2,1)}, bf16[384,1536]{1,0:T(8,128)(2,1)}, u32[]{:S(2)}, u32[]{:S(2)}) collective-permute-start(bf16[384,1536]{1,0:T(8,128)(2,1)} %pad_maximum_fusion.6), channel_id=1, source_target_pairs={{0,4},{4,0},{8,12},{12,8},{16,20},{20,16},{24,28},{28,24},{1,5},{5... | collective-permute-start | bytes 3538952 | tf_op jit(solution)/shard_map/ppermute | solution.py:39
  111.4 36.1 %collective-permute-start.3 = (bf16[1024,768]{0,1:T(8,128)(2,1)S(1)}, bf16[1024,768]{0,1:T(8,128)(2,1)S(1)}, u32[]{:S(2)}, u32[]{:S(2)}) collective-permute-start(bf16[1024,768]{0,1:T(8,128)(2,1)S(1)} %pad_maximum_fusion.5), channel_id=1, source_target_pairs={{0,2},{2,0},{1,3},{3,1},{4,6},{6,4},{5,7},{7,5},{8,10},{10,8},{9,1... | collective-permute-start | bytes 4718600 | tf_op jit(solution)/shard_map/ppermute | solution.py:39
  114.1 28.5 %copy-start.23 = (bf16[768,1536]{1,0:T(8,128)(2,1)S(1)}, bf16[768,1536]{1,0:T(8,128)(2,1)}, u32[]{:S(2)}) copy-start(bf16[768,1536]{1,0:T(8,128)(2,1)} %constant_dynamic-update-slice_fusion.3) | copy-start | bytes 7077892
  191.0 6.1 %collective-permute-start.7 = (bf16[1024,768]{0,1:T(8,128)(2,1)S(1)}, bf16[1024,768]{0,1:T(8,128)(2,1)S(1)}, u32[]{:S(2)}, u32[]{:S(2)}) collective-permute-start(bf16[1024,768]{0,1:T(8,128)(2,1)S(1)} %convolution_convert_fusion.3), channel_id=1, source_target_pairs={{0,1},{1,0},{2,3},{3,2},{4,5},{5,4},{6,7},{7,6},{8,9},{9,8},{10,11... | collective-permute-start | bytes 4718600 | tf_op jit(solution)/shard_map/ppermute | solution.py:39
  219.3 28.7 %collective-permute-start.30 = (bf16[2,2,2,1,48,1536]{5,4,3,2,1,0:T(8,128)(2,1)}, bf16[2,2,2,1,48,1536]{5,4,3,2,1,0:T(8,128)(2,1)}, u32[]{:S(2)}, u32[]{:S(2)}) collective-permute-start(bf16[2,2,2,1,48,1536]{5,4,3,2,1,0:T(8,128)(2,1)} %constant_dynamic-slice_fusion.17), channel_id=1, source_target_pairs={{0,2},{2,0},{1,3},{3,1},{4,6},{6,4},{5,7},{7,5},{8,10},{10,8},{9,1... | collective-permute-start | bytes 3538952 | tf_op jit(solution)/shard_map/ppermute | solution.py:39
  220.8 35.2 %collective-permute-start.15 = (bf16[1024,768]{0,1:T(8,128)(2,1)S(1)}, bf16[1024,768]{0,1:T(8,128)(2,1)}, u32[]{:S(2)}, u32[]{:S(2)}) collective-permute-start(bf16[1024,768]{0,1:T(8,128)(2,1)S(1)} %convolution_convert_fusion.4), channel_id=1, source_target_pairs={{0,1},{1,0},{2,3},{3,2},{4,5},{5,4},{6,7},{7,6},{8,9},{9,8},{10,11... | collective-permute-start | bytes 4718600 | tf_op jit(solution)/shard_map/ppermute | solution.py:39
  222.2 29.2 %collective-permute-start.26 = (bf16[2,2,1,2,48,1536]{5,4,3,2,1,0:T(8,128)(2,1)}, bf16[2,2,1,2,48,1536]{5,4,3,2,1,0:T(8,128)(2,1)}, u32[]{:S(2)}, u32[]{:S(2)}) collective-permute-start(bf16[2,2,1,2,48,1536]{5,4,3,2,1,0:T(8,128)(2,1)} %constant_dynamic-slice_fusion.13), channel_id=1, source_target_pairs={{0,4},{4,0},{8,12},{12,8},{16,20},{20,16},{24,28},{28,24},{1,5},{5... | collective-permute-start | bytes 3538952 | tf_op jit(solution)/shard_map/ppermute | solution.py:39
  227.4 32.1 %collective-permute-start.14 = (bf16[1024,768]{0,1:T(8,128)(2,1)}, bf16[1024,768]{0,1:T(8,128)(2,1)S(1)}, u32[]{:S(2)}, u32[]{:S(2)}) collective-permute-start(bf16[1024,768]{0,1:T(8,128)(2,1)} %convolution_convert_fusion.5), channel_id=1, source_target_pairs={{0,1},{1,0},{2,3},{3,2},{4,5},{5,4},{6,7},{7,6},{8,9},{9,8},{10,11... | collective-permute-start | bytes 4718600 | tf_op jit(solution)/shard_map/ppermute | solution.py:39
  250.9 93.1 %collective-permute-start.31 = (bf16[2,2,1,1,48,1536]{5,4,3,2,1,0:T(8,128)(2,1)}, bf16[2,2,1,1,48,1536]{5,4,3,2,1,0:T(8,128)(2,1)}, u32[]{:S(2)}, u32[]{:S(2)}) collective-permute-start(bf16[2,2,1,1,48,1536]{5,4,3,2,1,0:T(8,128)(2,1)} %constant_dynamic-slice_fusion.18), channel_id=1, source_target_pairs={{0,4},{4,0},{8,12},{12,8},{16,20},{20,16},{24,28},{28,24},{1,5},{5... | collective-permute-start | bytes 1769480 | tf_op jit(solution)/shard_map/ppermute | solution.py:39
  254.4 180.3 %collective-permute-start.27 = (bf16[2,2,1,1,48,1536]{5,4,3,2,1,0:T(8,128)(2,1)}, bf16[2,2,1,1,48,1536]{5,4,3,2,1,0:T(8,128)(2,1)}, u32[]{:S(2)}, u32[]{:S(2)}) collective-permute-start(bf16[2,2,1,1,48,1536]{5,4,3,2,1,0:T(8,128)(2,1)} %constant_dynamic-slice_fusion.14), channel_id=1, source_target_pairs={{0,2},{2,0},{1,3},{3,1},{4,6},{6,4},{5,7},{7,5},{8,10},{10,8},{9,1... | collective-permute-start | bytes 1769480 | tf_op jit(solution)/shard_map/ppermute | solution.py:39
  272.7 55.4 %copy-start.63 = (f32[768]{0:T(1024)S(1)}, f32[768]{0:T(1024)}, u32[]{:S(2)}) copy-start(f32[768]{0:T(1024)} %get-tuple-element.377) | copy-start | bytes 9220
  331.9 104.0 %collective-permute-start.22 = (bf16[2,2,2,1,48,384]{5,4,3,2,1,0:T(8,128)(2,1)}, bf16[2,2,2,1,48,384]{5,4,3,2,1,0:T(8,128)(2,1)S(1)}, u32[]{:S(2)}, u32[]{:S(2)}) collective-permute-start(bf16[2,2,2,1,48,384]{5,4,3,2,1,0:T(8,128)(2,1)} %constant_dynamic-slice_fusion.8), channel_id=1, source_target_pairs={{0,2},{2,0},{1,3},{3,1},{4,6},{6,4},{5,7},{7,5},{8,10},{10,8},{9,1... | collective-permute-start | bytes 884744 | tf_op jit(solution)/shard_map/ppermute | solution.py:39
  339.0 120.0 %collective-permute-start.16 = (bf16[1,1024,768]{2,1,0:T(8,128)(2,1)}, bf16[1,1024,768]{2,1,0:T(8,128)(2,1)}, u32[]{:S(2)}, u32[]{:S(2)}) collective-permute-start(bf16[1,1024,768]{2,1,0:T(8,128)(2,1)} %fusion.72), channel_id=1, source_target_pairs={{0,2},{2,0},{1,3},{3,1},{4,6},{6,4},{5,7},{7,5},{8,10},{10,8},{9,1... | collective-permute-start | bytes 4718600 | tf_op jit(solution)/shard_map/ppermute | solution.py:39
  344.0 90.7 %copy-start.18 = (bf16[2,2,1,2,48,1536]{5,4,3,2,1,0:T(8,128)(2,1)S(1)}, bf16[2,2,1,2,48,1536]{5,4,3,2,1,0:T(8,128)(2,1)}, u32[]{:S(2)}) copy-start(bf16[2,2,1,2,48,1536]{5,4,3,2,1,0:T(8,128)(2,1)} %copy-done.17) | copy-start | bytes 3538948
  344.0 91.9 %copy-start.31 = (bf16[768,384]{1,0:T(8,128)(2,1)S(1)}, bf16[768,384]{1,0:T(8,128)(2,1)}, u32[]{:S(2)}) copy-start(bf16[768,384]{1,0:T(8,128)(2,1)} %convolution_convert_fusion.7) | copy-start | bytes 1769476
  345.6 97.0 %collective-permute-start.32 = (bf16[2,1,1,1,48,1536]{5,4,3,2,1,0:T(8,128)(2,1)S(1)}, bf16[2,1,1,1,48,1536]{5,4,3,2,1,0:T(8,128)(2,1)S(1)}, u32[]{:S(2)}, u32[]{:S(2)}) collective-permute-start(bf16[2,1,1,1,48,1536]{5,4,3,2,1,0:T(8,128)(2,1)S(1)} %constant_dynamic-slice_fusion.19), channel_id=1, source_target_pairs={{0,8},{4,12},{8,0},{12,4},{16,24},{20,28},{24,16},{28,20},{1,9},{5... | collective-permute-start | bytes 884744 | tf_op jit(solution)/shard_map/ppermute | solution.py:39
  436.0 5.2 collective-permute-start.23
  437.4 13.6 %collective-permute-start.28 = (bf16[2,1,1,1,48,1536]{5,4,3,2,1,0:T(8,128)(2,1)S(1)}, bf16[2,1,1,1,48,1536]{5,4,3,2,1,0:T(8,128)(2,1)S(1)}, u32[]{:S(2)}, u32[]{:S(2)}) collective-permute-start(bf16[2,1,1,1,48,1536]{5,4,3,2,1,0:T(8,128)(2,1)S(1)} %constant_dynamic-slice_fusion.15), channel_id=1, source_target_pairs={{0,8},{4,12},{8,0},{12,4},{16,24},{20,28},{24,16},{28,20},{1,9},{5... | collective-permute-start | bytes 884744 | tf_op jit(solution)/shard_map/ppermute | solution.py:39
  441.3 10.5 %collective-permute-start.24 = (bf16[2,1,1,1,48,384]{5,4,3,2,1,0:T(8,128)(2,1)S(1)}, bf16[2,1,1,1,48,384]{5,4,3,2,1,0:T(8,128)(2,1)S(1)}, u32[]{:S(2)}, u32[]{:S(2)}) collective-permute-start(bf16[2,1,1,1,48,384]{5,4,3,2,1,0:T(8,128)(2,1)S(1)} %constant_dynamic-slice_fusion.6), channel_id=1, source_target_pairs={{0,8},{4,12},{8,0},{12,4},{16,24},{20,28},{24,16},{28,20},{1,9},{5... | collective-permute-start | bytes 221192 | tf_op jit(solution)/shard_map/ppermute | solution.py:39
  443.5 32.7 %collective-permute-start.33 = (bf16[1,1,1,1,48,1536]{5,4,3,2,1,0:T(8,128)(2,1)}, bf16[1,1,1,1,48,1536]{5,4,3,2,1,0:T(8,128)(2,1)}, u32[]{:S(2)}, u32[]{:S(2)}) collective-permute-start(bf16[1,1,1,1,48,1536]{5,4,3,2,1,0:T(8,128)(2,1)} %constant_dynamic-slice_fusion.20), channel_id=1, source_target_pairs={{0,16},{4,20},{8,24},{12,28},{16,0},{20,4},{24,8},{28,12},{1,17},{... | collective-permute-start | bytes 442376 | tf_op jit(solution)/shard_map/ppermute | solution.py:39
  451.9 6.5 %collective-permute-start.25 = (bf16[1,1,1,1,48,384]{5,4,3,2,1,0:T(8,128)(2,1)S(1)}, bf16[1,1,1,1,48,384]{5,4,3,2,1,0:T(8,128)(2,1)S(1)}, u32[]{:S(2)}, u32[]{:S(2)}) collective-permute-start(bf16[1,1,1,1,48,384]{5,4,3,2,1,0:T(8,128)(2,1)S(1)} %constant_dynamic-slice_fusion.5), channel_id=1, source_target_pairs={{0,16},{4,20},{8,24},{12,28},{16,0},{20,4},{24,8},{28,12},{1,17},{... | collective-permute-start | bytes 110600 | tf_op jit(solution)/shard_map/ppermute | solution.py:39
  452.0 41.3 %collective-permute-start.29 = (bf16[1,1,1,1,48,1536]{5,4,3,2,1,0:T(8,128)(2,1)S(1)}, bf16[1,1,1,1,48,1536]{5,4,3,2,1,0:T(8,128)(2,1)}, u32[]{:S(2)}, u32[]{:S(2)}) collective-permute-start(bf16[1,1,1,1,48,1536]{5,4,3,2,1,0:T(8,128)(2,1)S(1)} %constant_dynamic-slice_fusion.16), channel_id=1, source_target_pairs={{0,16},{4,20},{8,24},{12,28},{16,0},{20,4},{24,8},{28,12},{1,17},{... | collective-permute-start | bytes 442376 | tf_op jit(solution)/shard_map/ppermute | solution.py:39
  474.0 17.2 %collective-permute-start.18 = (bf16[2,2,2,1,48,1152]{5,4,3,2,1,0:T(8,128)(2,1)S(1)}, bf16[2,2,2,1,48,1152]{5,4,3,2,1,0:T(8,128)(2,1)S(1)}, u32[]{:S(2)}, u32[]{:S(2)}) collective-permute-start(bf16[2,2,2,1,48,1152]{5,4,3,2,1,0:T(8,128)(2,1)S(1)} %constant_dynamic-slice_fusion.12), channel_id=1, source_target_pairs={{0,2},{2,0},{1,3},{3,1},{4,6},{6,4},{5,7},{7,5},{8,10},{10,8},{9,1... | collective-permute-start | bytes 2654216 | tf_op jit(solution)/shard_map/ppermute | solution.py:39
  482.9 26.5 %copy-start.11 = (bf16[1024,768]{1,0:T(8,128)(2,1)S(1)}, bf16[1024,768]{1,0:T(8,128)(2,1)}, u32[]{:S(2)}) copy-start(bf16[1024,768]{1,0:T(8,128)(2,1)} %copy-done.10) | copy-start | bytes 4718596
  482.9 30.5 %collective-permute-start.17 = (bf16[1024,768]{0,1:T(8,128)(2,1)}, bf16[1024,768]{0,1:T(8,128)(2,1)}, u32[]{:S(2)}, u32[]{:S(2)}) collective-permute-start(bf16[1024,768]{0,1:T(8,128)(2,1)} %bitcast_convert_fusion), channel_id=1, source_target_pairs={{0,1},{1,0},{2,3},{3,2},{4,5},{5,4},{6,7},{7,6},{8,9},{9,8},{10,11... | collective-permute-start | bytes 4718600 | tf_op jit(solution)/shard_map/ppermute | solution.py:39
  491.5 8.4 %collective-permute-start.19 = (bf16[2,2,1,1,48,1152]{5,4,3,2,1,0:T(8,128)(2,1)S(1)}, bf16[2,2,1,1,48,1152]{5,4,3,2,1,0:T(8,128)(2,1)S(1)}, u32[]{:S(2)}, u32[]{:S(2)}) collective-permute-start(bf16[2,2,1,1,48,1152]{5,4,3,2,1,0:T(8,128)(2,1)S(1)} %constant_dynamic-slice_fusion.11), channel_id=1, source_target_pairs={{0,4},{4,0},{8,12},{12,8},{16,20},{20,16},{24,28},{28,24},{1,5},{5... | collective-permute-start | bytes 1327112 | tf_op jit(solution)/shard_map/ppermute | solution.py:39
  500.0 13.3 %collective-permute-start.20 = (bf16[2,1,1,1,48,1152]{5,4,3,2,1,0:T(8,128)(2,1)S(1)}, bf16[2,1,1,1,48,1152]{5,4,3,2,1,0:T(8,128)(2,1)S(1)}, u32[]{:S(2)}, u32[]{:S(2)}) collective-permute-start(bf16[2,1,1,1,48,1152]{5,4,3,2,1,0:T(8,128)(2,1)S(1)} %constant_dynamic-slice_fusion.10), channel_id=1, source_target_pairs={{0,8},{4,12},{8,0},{12,4},{16,24},{20,28},{24,16},{28,20},{1,9},{5... | collective-permute-start | bytes 663560 | tf_op jit(solution)/shard_map/ppermute | solution.py:39
  517.5 4.2 collective-permute-start.34
  518.4 26.1 %collective-permute-start.21 = (bf16[1,1,1,1,48,1152]{5,4,3,2,1,0:T(8,128)(2,1)S(1)}, bf16[1,1,1,1,48,1152]{5,4,3,2,1,0:T(8,128)(2,1)S(1)}, u32[]{:S(2)}, u32[]{:S(2)}) collective-permute-start(bf16[1,1,1,1,48,1152]{5,4,3,2,1,0:T(8,128)(2,1)S(1)} %constant_dynamic-slice_fusion.9), channel_id=1, source_target_pairs={{0,16},{4,20},{8,24},{12,28},{16,0},{20,4},{24,8},{28,12},{1,17},{... | collective-permute-start | bytes 331784 | tf_op jit(solution)/shard_map/ppermute | solution.py:39
  521.7 3.7 collective-permute-start.35
  525.4 3.7 collective-permute-start.36
  529.1 12.2 %collective-permute-start.37 = (f32[1,1,1,1,1,432]{5,4,3,2,1,0:T(1,128)S(1)}, f32[1,1,1,1,1,432]{5,4,3,2,1,0:T(1,128)S(1)}, u32[]{:S(2)}, u32[]{:S(2)}) collective-permute-start(f32[1,1,1,1,1,432]{5,4,3,2,1,0:T(1,128)S(1)} %constant_dynamic-slice_fusion.28), channel_id=1, source_target_pairs={{0,16},{4,20},{8,24},{12,28},{16,0},{20,4},{24,8},{28,12},{1,17},{... | collective-permute-start | bytes 5192 | tf_op jit(solution)/shard_map/ppermute | solution.py:39
  (66 other events, 352.9 us)
